TPU v7x, 128 devices: a whole 4x4x4 slice. The times are simulated.
128 devices in a mesh: row: 8 (over x, core), col: 16 (over y, z).
Axes of the slice: x: 4, y: 4, z: 4, core: 2. Of those that a mesh axis runs over, the one named last changes fastest.
Arguments:
- root_inverse: float32 [4096, 4096], P('row', 'col'), as said below
- factor_one: float32 [16, 1024, 192], P('row'), may hold values from -0.1875 to 0.1875
- pivot_one: float32 [16, 192, 192], P('row'), as said below
- pattern_one: int32 [16, 16], P('row'), may hold values from 0 to 63, as said below
- factor_two: float32 [16, 16, 384, 192], P('row', 'col'), may hold values from -0.3125 to 0.3125
- pivot_two: float32 [16, 16, 192, 192], P('row', 'col'), as said below
- pattern_two: int32 [16, 16, 6], P('row'), may hold values from 0 to 18, as said below
Outputs:
- column_one: float32 [16, 1024, 192], P('row')
- diagonal_one: float32 [16, 192, 192], P('row')
- column_two: float32 [16, 16, 384, 192], P('row', 'col')
- diagonal_two: float32 [16, 16, 192, 192], P('row', 'col')
Inputs may be any that keep to these rules, and one draw needn't show every extreme that they name: `root_inverse`: symmetric. `pivot_one`: symmetric. `pivot_two`: symmetric. `pattern_one`: each row holds 16 different blocks in increasing order. `pattern_two`: each row holds 6 different blocks in increasing order.
All inputs are finite; a program needn't handle non-finite values.
Results may differ from a plain program's by a relative error of at most 0.0003.
Values sent between devices are 32-bit elements; how exact they have to be, the bound alone decides.
No kernel may reach another device: no remote copies, remote signals or barrier semaphores. Data moves between devices by JAX's collectives and lax.ppermute only.
A program may use at most 128 MiB of HBM per device.

v0:
```python
import functools

import jax
import jax.numpy as jnp
from jax import lax
from jax.experimental import pallas as pl
from jax.experimental.pallas import tpu as pltpu
from jax.sharding import PartitionSpec as P

F32 = jnp.float32
BF16 = jnp.bfloat16
BLOCK = 64
WIDTH = 192
ONE = 16
TWO = 6
OWN = 3
COLS = 16
ROWS = 8
SLICE = 4
UNITS = [(k, m) for k in range(TWO) for m in range(k + 1)]
BAND = ONE * SLICE
CHILD_TOP = 3 * BAND
MESSAGE = 280
WIDE = TWO * BLOCK
VMEM = pl.BlockSpec(memory_space=pltpu.VMEM)
SMEM = pl.BlockSpec(memory_space=pltpu.SMEM)
ANY = pl.BlockSpec(memory_space=pl.ANY)
HBM = pl.BlockSpec(memory_space=pltpu.HBM)


def in_hbm(arrays):
    return [pltpu.with_memory_space_constraint(array, pltpu.HBM) for array in arrays]


def split(value):
    high = value.astype(BF16)
    low = (value - high.astype(F32)).astype(BF16)
    return high, low


def product(left, right, dims=((1,), (0,))):
    def one(a, b):
        return lax.dot_general(a, b, (dims, ((), ())), preferred_element_type=F32)

    (lh, ll), (rh, rl) = left, right
    return one(lh, rh) + (one(lh, rl) + one(ll, rh))


def pack_kernel(root_ref, out_ref, near, ready, sems):
    def fetch(n, tile):
        here, lanes = slice(BLOCK * n, BLOCK * n + BLOCK), slice(128 * tile, 128 * tile + 128)
        return pltpu.make_async_copy(
            root_ref.at[here, lanes], near.at[tile, here], sems.at[0, n, tile]
        )

    def store(n):
        return pltpu.make_async_copy(ready.at[n], out_ref.at[:, n], sems.at[1, n, 0])

    for n in range(8):
        for tile in range(2):
            fetch(n, tile).start()
    for n in range(8):
        for tile in range(2):
            fetch(n, tile).wait()
            for place in range(COLS):
                ready[n, place, :, 128 * tile : 128 * tile + 128] = near[
                    tile, pl.ds(BLOCK * n + place, SLICE, stride=16), :
                ]
        store(n).start()
    for n in range(8):
        store(n).wait()


def pack(root):
    return pl.pallas_call(
        pack_kernel,
        out_shape=pltpu.HBM((COLS, 8, SLICE, 256), F32),
        in_specs=[HBM],
        out_specs=HBM,
        scratch_shapes=[
            pltpu.VMEM((2, 512, 128), F32),
            pltpu.VMEM((8, COLS, SLICE, 256), F32),
            pltpu.SemaphoreType.DMA((2, 8, 2)),
        ],
        name="pack",
    )(*in_hbm([root]))


def pick_lanes(one_ref, parent, pair, side):
    block = one_ref[parent, 2 * pair + side]
    lanes = pl.ds(pl.multiple_of(((block >> 1) & 1) << 7, 128), 128)
    return block >> 2, lanes, ((block & 1) ^ side) << 6


def source_of(place_ref, block):
    return (((block >> 4) - place_ref[0]) & 3), ((block >> 3) & 1) == place_ref[1]


ROWS_SHAPE = (2, ONE, SLICE, ONE * BLOCK)


def early_kernel(
    place_ref, one_ref, other_ref, own_ref, low_ref, high_ref, far_factor,
    mine_out, other_out, split_high, split_low, rows, factor_ref, sem,
):
    left_half = lax.broadcasted_iota(jnp.int32, (ONE, SLICE, 128), 2) < BLOCK
    factor_copy = pltpu.make_async_copy(far_factor, factor_ref, sem)
    factor_copy.start()
    patterns = [(one_ref, 0), (one_ref, 1), (other_ref, 0), (other_ref, 1)]

    def row_step(a, carry):
        for parent, (pattern, n) in enumerate(patterns):
            block = pattern[n, a]
            step, here = source_of(place_ref, block)
            high = (block >> 2) & 1

            @pl.when(here)
            def _():
                @pl.when(step == 0)
                def _():
                    rows[parent, a] = own_ref[:, block & 7]

                @pl.when((step == 3) & (high == 0))
                def _():
                    rows[parent, a] = low_ref[:, block & 3]

                @pl.when((step == 1) & (high == 1))
                def _():
                    rows[parent, a] = high_ref[:, block & 3]

        return carry

    lax.fori_loop(0, ONE, row_step, 0)
    for parent, (pattern, n) in enumerate(patterns):
        for pair in range(ONE // 2):
            halves = []
            for side in range(2):
                source, lanes, turn = pick_lanes(pattern, n, pair, side)
                halves.append(pltpu.roll(rows[parent, :, source, :, lanes], turn, 2))
            lanes = slice(pair * 128, pair * 128 + 128)
            out = (mine_out, other_out)[parent // 2]
            out[n, :, :, lanes] = jnp.where(left_half, halves[0], halves[1])
    factor_copy.wait()
    for parent in range(2):
        split_high[parent], split_low[parent] = split(factor_ref[parent])


def early(place, pattern_one, pattern_other, factor, pieces):
    band = jax.ShapeDtypeStruct(ROWS_SHAPE, F32)
    halves = jax.ShapeDtypeStruct(factor.shape, BF16)
    return pl.pallas_call(
        early_kernel,
        out_shape=(band, band, halves, halves),
        in_specs=[SMEM] * 3 + [VMEM] * 3 + [HBM],
        out_specs=(VMEM,) * 4,
        scratch_shapes=[
            pltpu.VMEM((4, ONE, COLS, SLICE, 256), F32),
            pltpu.VMEM(factor.shape, F32),
            pltpu.SemaphoreType.DMA,
        ],
        compiler_params=pltpu.CompilerParams(vmem_limit_bytes=20 * 2**20),
        cost_estimate=pl.CostEstimate(flops=0, bytes_accessed=12 * 2**20, transcendentals=0),
        name="early",
    )(place, pattern_one, pattern_other, *pieces, *in_hbm([factor]))


def fill_kernel(whence, place_ref, *refs):
    count = (len(refs) - len(whence)) // 3
    patterns, bands, outs = refs[:count], refs[count : 2 * count], refs[-count:]
    pieces = refs[2 * count : -count]
    left_half = lax.broadcasted_iota(jnp.int32, (SLICE, 128), 1) < BLOCK
    for band, out in zip(bands, outs):
        out[...] = band[...]

    def row_step(a, carry):
        for pattern, out in zip(patterns, outs):
            for parent in range(2):
                block = pattern[parent, a]
                step, here = source_of(place_ref, block)
                high = (block >> 2) & 1

                def fill(piece):
                    for pair in range(ONE // 2):
                        halves = []
                        for side in range(2):
                            source, lanes, turn = pick_lanes(pattern, parent, pair, side)
                            halves.append(pltpu.roll(piece[source, block & 3, :, lanes], turn, 1))
                        lanes = slice(pair * 128, pair * 128 + 128)
                        out[parent, a, :, lanes] = jnp.where(left_half, halves[0], halves[1])

                for (place, half), piece in zip(whence, pieces):

                    @pl.when(here & (step == place) & (high == half))
                    def _():
                        fill(piece)

        return carry

    lax.fori_loop(0, ONE, row_step, 0)


def fill(name, whence, place, patterns, bands, pieces):
    count = len(bands)
    return pl.pallas_call(
        functools.partial(fill_kernel, whence),
        out_shape=(jax.ShapeDtypeStruct(ROWS_SHAPE, F32),) * count,
        in_specs=[SMEM] * (1 + count) + [VMEM] * (count + len(pieces)),
        out_specs=(VMEM,) * count,
        compiler_params=pltpu.CompilerParams(vmem_limit_bytes=20 * 2**20),
        cost_estimate=pl.CostEstimate(flops=0, bytes_accessed=3 * 2**20, transcendentals=0),
        name=name,
    )(place, *patterns, *bands, *pieces)


def select_kernel(
    place_ref, one_ref, two_ref, high_ref, low_ref, mine_ref, other_ref, out_ref, band, ready, sems
):
    left_half = lax.broadcasted_iota(jnp.int32, (SLICE, 128), 1) < BLOCK

    for parent in range(2):
        for a in range(ONE):
            here = source_of(place_ref, one_ref[parent, a])[1]
            for pair in range(ONE // 2):
                lanes = slice(pair * 128, pair * 128 + 128)
                value = jnp.where(
                    here, mine_ref[parent, a, :, lanes], other_ref[parent, a, :, lanes]
                )
                band[0, parent, a, :, lanes] = value
                band[1, parent, a, :, lanes] = pltpu.roll(value, BLOCK, 1)
    columns = jnp.concatenate(
        [
            -product(
                split(band[0, parent].reshape(BAND, ONE * BLOCK)),
                (high_ref[parent], low_ref[parent]),
                ((1,), (1,)),
            )
            for parent in range(2)
        ],
        axis=1,
    )
    for child in range(COLS):
        for tile in range(3):
            ready[child, tile * BAND : tile * BAND + BAND, :] = columns[
                :, 128 * tile : 128 * tile + 128
            ]

    def send(n):
        children = slice(0, COLS) if n == 0 else slice(8 * (n - 1), 8 * n)
        part = slice(0, CHILD_TOP) if n == 0 else slice(CHILD_TOP, MESSAGE)
        return pltpu.make_async_copy(
            ready.at[children, part], out_ref.at[children, part], sems.at[n]
        )

    def child_step(child, carry):
        picks = [
            [jnp.maximum(two_ref[parent, child, n] - OWN, 0) for n in range(TWO)]
            for parent in range(2)
        ]
        for unit, (k, m) in enumerate(UNITS):
            halves = []
            for parent in range(2):
                row, block = picks[parent][k], picks[parent][m]
                lanes = pl.ds(pl.multiple_of((block >> 1) << 7, 128), 128)
                halves.append(band[(block & 1) ^ parent, parent, row, :, lanes])
            top = CHILD_TOP + unit * SLICE
            ready[child, top : top + SLICE, :] = jnp.where(left_half, halves[0], halves[1])
        return carry

    send(0).start()
    lax.fori_loop(0, 8, child_step, 0, unroll=4)
    send(1).start()
    lax.fori_loop(8, COLS, child_step, 0, unroll=4)
    send(2).start()
    for n in range(3):
        send(n).wait()


def select(place, pattern_one, pattern_two, high, low, mine, other):
    return pl.pallas_call(
        select_kernel,
        out_shape=pltpu.HBM((COLS, MESSAGE, 128), F32),
        in_specs=[SMEM] * 3 + [VMEM] * 4,
        out_specs=HBM,
        scratch_shapes=[
            pltpu.VMEM((2,) + ROWS_SHAPE, F32),
            pltpu.VMEM((COLS, MESSAGE, 128), F32),
            pltpu.SemaphoreType.DMA((3,)),
        ],
        compiler_params=pltpu.CompilerParams(vmem_limit_bytes=20 * 2**20),
        name="select",
    )(place, pattern_one, pattern_two, high, low, mine, other)


def final_kernel(two_ref, got_ref, *refs):
    (far_in, far_out, beside, chosen, near_in, near_out, sems) = (
        refs[:4], refs[4:8], refs[8:10], refs[10:12], refs[12:16], refs[16:20], refs[20],
    )
    factor_ref, child_factor_ref, pivot_ref, child_pivot_ref = near_in
    column_ref, diagonal_ref, child_column_ref, child_diagonal_ref = near_out
    fetches = [
        pltpu.make_async_copy(far, near, sems.at[n])
        for n, (far, near) in enumerate(zip(far_in, near_in))
    ]
    stores = [
        [
            pltpu.make_async_copy(near.at[parent], far.at[parent], sems.at[4 + 2 * n + parent])
            for parent in range(2)
        ]
        for n, (far, near) in enumerate(zip(far_out, near_out))
    ]
    for fetch in fetches:
        fetch.start()
    left_half = lax.broadcasted_iota(jnp.int32, (16, 128), 1) < BLOCK
    left_block = lax.broadcasted_iota(jnp.int32, (BLOCK, 128), 1) < BLOCK
    nt = ((1,), (1,))
    for n in range(BAND):
        tiles = [got_ref[pl.ds(m * BAND + n, 16, stride=MESSAGE), :] for m in range(3)]
        here = slice(WIDTH + 16 * n, WIDTH + 16 * n + 16)
        turned = [pltpu.roll(tile, BLOCK, 1) for tile in tiles[1:]]
        beside[0][here, 0:128] = tiles[0]
        beside[0][here, 128:256] = tiles[1]
        beside[1][here, 0:128] = jnp.where(left_half, turned[0], turned[1])
        beside[1][here, 128:256] = turned[1]
    for parent in range(2):
        column_ref[parent] = beside[parent][WIDTH:, 0:WIDTH].T
        stores[0][parent].start()
    for unit, (k, m) in enumerate(UNITS):
        for n in range(SLICE):
            value = got_ref[pl.ds(CHILD_TOP + unit * SLICE + n, 16, stride=MESSAGE), :]
            turned = pltpu.roll(value, BLOCK, 1)
            here = slice(BLOCK * k + 16 * n, BLOCK * k + 16 * n + 16)
            lanes = slice(BLOCK * m, BLOCK * m + BLOCK)
            half = slice(0, BLOCK) if m % 2 == 0 else slice(BLOCK, 128)
            chosen[m % 2][here, lanes] = value[:, half]
            chosen[1 - m % 2][here, lanes] = turned[:, half]
    fetches[0].wait()
    fetches[2].wait()
    diagonals = [
        pivot_ref[parent]
        - product(split(factor_ref[parent]), split(beside[parent][WIDTH:, 0:WIDTH]))
        for parent in range(2)
    ]
    for parent in range(2):
        diagonal_ref[parent] = diagonals[parent]
        beside[parent][0:WIDTH, 0:WIDTH] = diagonals[parent]
    for parent in range(2):
        stores[1][parent].start()
    row_block = lax.broadcasted_iota(jnp.int32, (WIDE, WIDE), 0) // BLOCK
    lane_block = lax.broadcasted_iota(jnp.int32, (WIDE, WIDE), 1) // BLOCK
    for parent in range(2):
        picks = [two_ref[parent, n] for n in range(TWO)]
        for k in range(TWO):
            here = slice(BLOCK * k, BLOCK * k + BLOCK)
            rows = pl.ds(pl.multiple_of(picks[k] << 6, BLOCK), BLOCK)
            tiles = [beside[parent][rows, 128 * n : 128 * n + 128] for n in range(2)]
            turned = [pltpu.roll(tile, BLOCK, 1) for tile in tiles]
            even = jnp.where(
                picks[0] == 0, tiles[0], jnp.where(picks[0] == 1, turned[0], tiles[1])
            )
            odd = jnp.where(picks[1] == 1, tiles[0], turned[1])
            near = chosen[parent][here, 0:128]
            chosen[parent][here, 0:128] = jnp.where(
                left_block,
                jnp.where(picks[0] >= OWN, near, even),
                jnp.where(picks[1] >= OWN, near, odd),
            )
            if k >= 2:
                near = chosen[parent][here, 128:256]
                chosen[parent][here, 128:256] = jnp.where(
                    left_block & (picks[2] < OWN), tiles[1], near
                )
    fetches[1].wait()
    fetches[3].wait()
    factors = [split(child_factor_ref[parent, 0]) for parent in range(2)]
    results = []
    for parent in range(2):
        lower = chosen[parent][...]
        whole = jnp.where(row_block >= lane_block, lower, lower.T)
        results.append(-product(factors[parent], split(whole)))
    for parent in range(2):
        child_column_ref[parent, 0] = results[parent]
    for parent in range(2):
        stores[2][parent].start()
    diagonals = [
        child_pivot_ref[parent, 0] - product(factors[parent], split(results[parent]), nt)
        for parent in range(2)
    ]
    for parent in range(2):
        child_diagonal_ref[parent, 0] = diagonals[parent]
    for parent in range(2):
        stores[3][parent].start()
    for pair in stores:
        for store in pair:
            store.wait()


def finish(own_two, got, arrays):
    shapes = (
        (2, WIDTH, ONE * BLOCK),
        (2, WIDTH, WIDTH),
        (2, 1, WIDTH, WIDE),
        (2, 1, WIDTH, WIDTH),
    )
    return pl.pallas_call(
        final_kernel,
        out_shape=tuple(pltpu.HBM(shape, F32) for shape in shapes),
        in_specs=[SMEM, VMEM] + [HBM] * 4,
        out_specs=(HBM,) * 4,
        scratch_shapes=[pltpu.VMEM((WIDTH + ONE * BLOCK, 256), F32)] * 2
        + [pltpu.VMEM((WIDE, WIDE), F32)] * 2
        + [pltpu.VMEM(array.shape, array.dtype) for array in arrays]
        + [pltpu.VMEM(shape, F32) for shape in shapes]
        + [pltpu.SemaphoreType.DMA((12,))],
        compiler_params=pltpu.CompilerParams(vmem_limit_bytes=24 * 2**20),
        name="finish",
    )(own_two, got, *in_hbm(arrays))


FORWARD = [(r, (r + 2) % ROWS) for r in range(ROWS)]
BACKWARD = [(r, (r - 2) % ROWS) for r in range(ROWS)]
SWAP = [(r, r ^ 1) for r in range(ROWS)]


def per_device(
    root_inverse, factor_one, pivot_one, pattern_one, factor_two, pivot_two, pattern_two
):
    row = lax.axis_index("row")
    place = jnp.stack([row >> 1, row & 1]).astype(jnp.int32)
    col = lax.axis_index("col")
    pattern_other = lax.ppermute(pattern_one, "row", SWAP)
    factor_one = jnp.swapaxes(factor_one, 1, 2)
    factor_two = jnp.swapaxes(factor_two, 2, 3)
    shard = lax.all_to_all(pack(root_inverse), "col", 0, 0, tiled=True)
    shard, pattern_other = lax.optimization_barrier((shard, pattern_other))
    halves = [shard[:, :4], shard[:, 4:]]
    behind = [lax.ppermute(half, "row", FORWARD) for half in halves]
    ahead = [lax.ppermute(half, "row", BACKWARD) for half in halves]
    across = [lax.ppermute(behind[0], "row", FORWARD), lax.ppermute(ahead[1], "row", BACKWARD)]
    mine, other, high, low = early(
        place, pattern_one, pattern_other, factor_one, [shard, behind[0], ahead[1]]
    )
    mine, other = fill(
        "second",
        ((1, 0), (3, 1)),
        place,
        (pattern_one, pattern_other),
        (mine, other),
        (ahead[0], behind[1]),
    )
    relayed = ((2, 0), (2, 1))
    (other,) = fill("last", relayed, place, (pattern_other,), (other,), across)
    other = lax.ppermute(other, "row", SWAP)
    (mine,) = fill("last", relayed, place, (pattern_one,), (mine,), across)
    message = select(place, pattern_one, pattern_two, high, low, mine, other)
    got = lax.all_to_all(message, "col", 0, 0, tiled=True)
    own_two = lax.dynamic_index_in_dim(pattern_two, col, 1, keepdims=False)
    column_one, diagonal_one, column_two, diagonal_two = finish(
        own_two,
        got.reshape(COLS * MESSAGE, 128),
        (factor_one, factor_two, pivot_one, pivot_two),
    )
    return (
        jnp.swapaxes(column_one, 1, 2),
        diagonal_one,
        jnp.swapaxes(column_two, 2, 3),
        diagonal_two,
    )


def solution(mesh):
    placed = (
        P("row", "col"),
        P("row", None, None),
        P("row", None, None),
        P("row", None),
        P("row", "col", None, None),
        P("row", "col", None, None),
        P("row", None, None),
    )
    return jax.shard_map(
        per_device,
        mesh=mesh,
        in_specs=placed,
        out_specs=(
            P("row", None, None),
            P("row", None, None),
            P("row", "col", None, None),
            P("row", "col", None, None),
        ),
        check_vma=False,
    )
```

profile of v0, /device:TPU:1, one launch (start us, length us, event | category | flops | bytes accessed | tf_op | source)
XLA Modules:
  0.0 95.7 jit_solution(17271719980506816165)
XLA Ops:
  0.6 0.0 copy-start
  0.6 1.9 %pack.1 = f32[16,8,4,256]{3,2,1,0:T(4,128)} custom-call(f32[512,256]{1,0:T(8,128)} %root_ref.1), custom_call_target="tpu_custom_call" | custom-call | tf_op jit(solution)/shard_map/pack/pallas_call | solution.py:75
  2.6 8.6 %all-to-all-start = ((f32[16,8,4,256]{3,2,1,0:T(4,128)}), f32[16,8,4,256]{3,2,1,0:T(4,128)S(1)}, u32[]{:S(2)}, u32[]{:S(2)}) async-start(f32[16,8,4,256]{3,2,1,0:T(4,128)} %pack.1), calls=%async_computation | async-start | bytes 1048576 | tf_op jit(solution)/shard_map/all_to_all | solution.py:433
  11.2 1.0 %collective-permute-start = (s32[2,16]{1,0:T(2,128)}, s32[2,16]{1,0:T(2,128)S(1)}, u32[]{:S(2)}, u32[]{:S(2)}) collective-permute-start(s32[2,16]{1,0:T(2,128)} %one_ref.3), channel_id=1, source_target_pairs={{0,16},{16,0},{32,48},{48,32},{64,80},{80,64},{96,112},{112,96},{1... | collective-permute-start | bytes 392 | tf_op jit(solution)/shard_map/ppermute | solution.py:430
  12.2 1.0 %collective-permute-done.other_ref.refs_1_.refs_0_ = s32[2,16]{1,0:T(2,128)S(1)} collective-permute-done((s32[2,16]{1,0:T(2,128)}, s32[2,16]{1,0:T(2,128)S(1)}, u32[]{:S(2)}, u32[]{:S(2)}) %collective-permute-start) | collective-permute-done | bytes 160 | tf_op jit(solution)/shard_map/ppermute | solution.py:430
  13.3 8.2 %all-to-all-done.own_ref = f32[16,8,4,256]{3,2,1,0:T(4,128)S(1)} async-done(((f32[16,8,4,256]{3,2,1,0:T(4,128)}), f32[16,8,4,256]{3,2,1,0:T(4,128)S(1)}, u32[]{:S(2)}, u32[]{:S(2)}) %all-to-all-start) | async-done | bytes 524320 | tf_op jit(solution)/shard_map/all_to_all | solution.py:433
  21.5 0.8 fusion
  22.3 2.5 %collective-permute-start.2 = (f32[16,4,4,256]{3,2,1,0:T(4,128)}, f32[16,4,4,256]{3,2,1,0:T(4,128)S(1)}, u32[]{:S(2)}, u32[]{:S(2)}) collective-permute-start(f32[16,4,4,256]{3,2,1,0:T(4,128)} %get-tuple-element.28), channel_id=1, source_target_pairs={{0,96},{16,112},{32,0},{48,16},{64,32},{80,48},{96,64},{112,80},{1... | collective-permute-start | bytes 786440 | tf_op jit(solution)/shard_map/ppermute | solution.py:437
  24.8 0.0 collective-permute-start.1
  24.8 0.2 collective-permute-start.4
  25.0 2.5 %collective-permute-start.3 = (f32[16,4,4,256]{3,2,1,0:T(4,128)}, f32[16,4,4,256]{3,2,1,0:T(4,128)}, u32[]{:S(2)}, u32[]{:S(2)}) collective-permute-start(f32[16,4,4,256]{3,2,1,0:T(4,128)} %get-tuple-element.29), channel_id=1, source_target_pairs={{0,96},{16,112},{32,0},{48,16},{64,32},{80,48},{96,64},{112,80},{1... | collective-permute-start | bytes 786440 | tf_op jit(solution)/shard_map/ppermute | solution.py:437
  27.5 1.1 %collective-permute-done.2.high_ref = f32[16,4,4,256]{3,2,1,0:T(4,128)S(1)} collective-permute-done((f32[16,4,4,256]{3,2,1,0:T(4,128)}, f32[16,4,4,256]{3,2,1,0:T(4,128)S(1)}, u32[]{:S(2)}, u32[]{:S(2)}) %collective-permute-start.2) | collective-permute-done | bytes 262176 | tf_op jit(solution)/shard_map/ppermute | solution.py:437
  28.6 3.3 %collective-permute-start.6 = (f32[16,4,4,256]{3,2,1,0:T(4,128)S(1)}, f32[16,4,4,256]{3,2,1,0:T(4,128)S(1)}, u32[]{:S(2)}, u32[]{:S(2)}) collective-permute-start(f32[16,4,4,256]{3,2,1,0:T(4,128)S(1)} %collective-permute-done.2.high_ref), channel_id=1, source_target_pairs={{0,96},{16,112},{32,0},{48,16},{64,32},{80,48},{96,64},{112,80},{1... | collective-permute-start | bytes 786440 | tf_op jit(solution)/shard_map/ppermute | solution.py:438
  31.9 0.0 collective-permute-done.1.low_ref
  31.9 0.0 collective-permute-start.5
  31.9 0.1 pad_add_fusion.place_ref
  32.0 0.0 copy-done
  32.0 0.0 copy-start.1
  32.0 3.2 %early.1 = (f32[2,16,4,1024]{3,2,1,0:T(4,128)S(1)}, f32[2,16,4,1024]{3,2,1,0:T(4,128)S(1)}, bf16[2,192,1024]{2,1,0:T(8,128)(2,1)S(1)}, bf16[2,192,1024]{2,1,0:T(8,128)(2,1)S(1)}) custom-call(s32[2]{0:T(128)S(1)} %pad_add_fusion.place_ref, s32[2,16]{1,0:T(2,128)S(1)} %copy-done, s32[2,16]{1,0:T(2,128)S(1)} %collective-permute-done.other_ref.refs_1_.refs_0_, ...), custom_call_target="tpu_custom_call" | custom-call | bytes 12582912 | tf_op jit(solution)/shard_map/early/pallas_call | solution.py:151
  35.2 2.0 %collective-permute-done.4.refs_5_ = f32[16,4,4,256]{3,2,1,0:T(4,128)S(1)} collective-permute-done((f32[16,4,4,256]{3,2,1,0:T(4,128)}, f32[16,4,4,256]{3,2,1,0:T(4,128)S(1)}, u32[]{:S(2)}, u32[]{:S(2)}) %collective-permute-start.4) | collective-permute-done | bytes 262176 | tf_op jit(solution)/shard_map/ppermute | solution.py:436
  37.2 0.0 collective-permute-done.3.refs_4_
  37.2 3.1 %second.1 = (f32[2,16,4,1024]{3,2,1,0:T(4,128)S(1)}, f32[2,16,4,1024]{3,2,1,0:T(4,128)S(1)}) custom-call(s32[2]{0:T(128)S(1)} %pad_add_fusion.place_ref, s32[2,16]{1,0:T(2,128)S(1)} %copy-done, s32[2,16]{1,0:T(2,128)S(1)} %collective-permute-done.other_ref.refs_1_.refs_0_, f32[2,16,4,1024]{3,2,1,0:T(4,128)S(1)} %get-tuple-element.20.refs_2_, ...), custom_call_target="tpu_custom_call" | custom-call | bytes 3145728 | tf_op jit(solution)/shard_map/second/pallas_call | solution.py:204
  40.3 0.0 collective-permute-done.6.refs_3_
  40.3 2.5 %collective-permute-done.5.refs_2_ = f32[16,4,4,256]{3,2,1,0:T(4,128)S(1)} collective-permute-done((f32[16,4,4,256]{3,2,1,0:T(4,128)S(1)}, f32[16,4,4,256]{3,2,1,0:T(4,128)S(1)}, u32[]{:S(2)}, u32[]{:S(2)}) %collective-permute-start.5) | collective-permute-done | bytes 262176 | tf_op jit(solution)/shard_map/ppermute | solution.py:438
  42.8 1.9 %last.3 = f32[2,16,4,1024]{3,2,1,0:T(4,128)S(1)} custom-call(s32[2]{0:T(128)S(1)} %pad_add_fusion.place_ref, s32[2,16]{1,0:T(2,128)S(1)} %collective-permute-done.other_ref.refs_1_.refs_0_, f32[2,16,4,1024]{3,2,1,0:T(4,128)S(1)} %get-tuple-element.23.refs_1_, f32[16,4,4,256]{3,2,1,0:T(4,128)S(1)} %collective-permute-done.5.refs_2_, ...), custom_call_target="tpu_custom_call" | custom-call | bytes 3145728 | tf_op jit(solution)/shard_map/last/pallas_call | solution.py:204
  44.7 4.1 %collective-permute-start.7 = (f32[2,16,4,1024]{3,2,1,0:T(4,128)S(1)}, f32[2,16,4,1024]{3,2,1,0:T(4,128)}, u32[]{:S(2)}, u32[]{:S(2)}) collective-permute-start(f32[2,16,4,1024]{3,2,1,0:T(4,128)S(1)} %last.3), channel_id=1, source_target_pairs={{0,16},{16,0},{32,48},{48,32},{64,80},{80,64},{96,112},{112,96},{1... | collective-permute-start | bytes 1572872 | tf_op jit(solution)/shard_map/ppermute | solution.py:452
  48.9 0.0 copy-done.1
  48.9 0.1 copy.12.two_ref
  49.0 1.5 %last.2.mine_ref = f32[2,16,4,1024]{3,2,1,0:T(4,128)S(1)} custom-call(s32[2]{0:T(128)S(1)} %pad_add_fusion.place_ref, s32[2,16]{1,0:T(2,128)S(1)} %copy-done, f32[2,16,4,1024]{3,2,1,0:T(4,128)S(1)} %get-tuple-element.22.refs_1_, f32[16,4,4,256]{3,2,1,0:T(4,128)S(1)} %collective-permute-done.5.refs_2_, f32[16,4,4,256]{3,2,1,0:T(4,128)S(1)} %collective-permute-done.6.refs_3_), custom_call_target="tpu_custom_call" | custom-call | bytes 3145728 | tf_op jit(solution)/shard_map/last/pallas_call | solution.py:204
  50.5 0.1 collective-permute-done.7.other_ref
  50.6 4.4 %select.1 = f32[16,280,128]{2,1,0:T(8,128)} custom-call(s32[2]{0:T(128)S(1)} %pad_add_fusion.place_ref, s32[2,16]{1,0:T(2,128)S(1)} %copy-done, s32[2,16,6]{2,1,0:T(8,128)S(1)} %copy.12.two_ref, bf16[2,192,1024]{2,1,0:T(8,128)(2,1)S(1)} %get-tuple-element.18.high_ref, bf16[2,192,1024]{2,1,0:T(8,128)(2,1)S(1)} %get-tuple-element.19.low_ref, ...), custom_call_target="tpu_custom_call" | custom-call | tf_op jit(solution)/shard_map/select/pallas_call | solution.py:279
  55.0 3.7 %all-to-all-start.1 = ((f32[16,280,128]{2,1,0:T(8,128)}), f32[16,280,128]{2,1,0:T(8,128)S(1)}, u32[]{:S(2)}, u32[]{:S(2)}) async-start(f32[16,280,128]{2,1,0:T(8,128)} %select.1), calls=%async_computation.1 | async-start | bytes 4587520 | tf_op jit(solution)/shard_map/all_to_all | solution.py:455
  58.7 0.1 constant_dynamic-slice_fusion
  58.8 0.1 copy.11
  58.9 31.1 %all-to-all-done.1 = f32[16,280,128]{2,1,0:T(8,128)S(1)} async-done(((f32[16,280,128]{2,1,0:T(8,128)}), f32[16,280,128]{2,1,0:T(8,128)S(1)}, u32[]{:S(2)}, u32[]{:S(2)}) %all-to-all-start.1) | async-done | bytes 2293792 | tf_op jit(solution)/shard_map/all_to_all | solution.py:455
  90.0 5.7 %finish.1 = (f32[2,192,1024]{2,1,0:T(8,128)}, f32[2,192,192]{2,1,0:T(8,128)}, f32[2,1,192,384]{3,2,1,0:T(8,128)}, f32[2,1,192,192]{3,2,1,0:T(8,128)}) custom-call(s32[2,6]{1,0:T(2,128)S(1)} %bitcast.9, f32[4480,128]{1,0:T(8,128)S(1)} %bitcast.8, f32[2,192,1024]{2,1,0:T(8,128)} %bitcast.11, f32[2,1,192,384]{3,2,1,0:T(8,128)} %bitcast.12, ...), custom_call_target="tpu_custom_call" | custom-call | tf_op jit(solution)/shard_map/finish/pallas_call | solution.py:404
Async XLA Ops:
  0.6 31.3 %copy-start = (s32[2,16]{1,0:T(2,128)S(1)}, s32[2,16]{1,0:T(2,128)}, u32[]{:S(2)}) copy-start(s32[2,16]{1,0:T(2,128)} %one_ref.3) | copy-start | bytes 388
  2.6 18.9 %all-to-all-start = ((f32[16,8,4,256]{3,2,1,0:T(4,128)}), f32[16,8,4,256]{3,2,1,0:T(4,128)S(1)}, u32[]{:S(2)}, u32[]{:S(2)}) async-start(f32[16,8,4,256]{3,2,1,0:T(4,128)} %pack.1), calls=%async_computation | async-start | bytes 1048576 | tf_op jit(solution)/shard_map/all_to_all | solution.py:433
  11.2 2.1 %collective-permute-start = (s32[2,16]{1,0:T(2,128)}, s32[2,16]{1,0:T(2,128)S(1)}, u32[]{:S(2)}, u32[]{:S(2)}) collective-permute-start(s32[2,16]{1,0:T(2,128)} %one_ref.3), channel_id=1, source_target_pairs={{0,16},{16,0},{32,48},{48,32},{64,80},{80,64},{96,112},{112,96},{1... | collective-permute-start | bytes 392 | tf_op jit(solution)/shard_map/ppermute | solution.py:430
  22.3 6.2 %collective-permute-start.2 = (f32[16,4,4,256]{3,2,1,0:T(4,128)}, f32[16,4,4,256]{3,2,1,0:T(4,128)S(1)}, u32[]{:S(2)}, u32[]{:S(2)}) collective-permute-start(f32[16,4,4,256]{3,2,1,0:T(4,128)} %get-tuple-element.28), channel_id=1, source_target_pairs={{0,96},{16,112},{32,0},{48,16},{64,32},{80,48},{96,64},{112,80},{1... | collective-permute-start | bytes 786440 | tf_op jit(solution)/shard_map/ppermute | solution.py:437
  24.8 7.1 %collective-permute-start.1 = (f32[16,4,4,256]{3,2,1,0:T(4,128)}, f32[16,4,4,256]{3,2,1,0:T(4,128)S(1)}, u32[]{:S(2)}, u32[]{:S(2)}) collective-permute-start(f32[16,4,4,256]{3,2,1,0:T(4,128)} %get-tuple-element.29), channel_id=1, source_target_pairs={{0,32},{16,48},{32,64},{48,80},{64,96},{80,112},{96,0},{112,16},{1... | collective-permute-start | bytes 786440 | tf_op jit(solution)/shard_map/ppermute | solution.py:436
  24.8 12.4 %collective-permute-start.4 = (f32[16,4,4,256]{3,2,1,0:T(4,128)}, f32[16,4,4,256]{3,2,1,0:T(4,128)S(1)}, u32[]{:S(2)}, u32[]{:S(2)}) collective-permute-start(f32[16,4,4,256]{3,2,1,0:T(4,128)} %get-tuple-element.28), channel_id=1, source_target_pairs={{0,32},{16,48},{32,64},{48,80},{64,96},{80,112},{96,0},{112,16},{1... | collective-permute-start | bytes 786440 | tf_op jit(solution)/shard_map/ppermute | solution.py:436
  25.0 12.2 %collective-permute-start.3 = (f32[16,4,4,256]{3,2,1,0:T(4,128)}, f32[16,4,4,256]{3,2,1,0:T(4,128)}, u32[]{:S(2)}, u32[]{:S(2)}) collective-permute-start(f32[16,4,4,256]{3,2,1,0:T(4,128)} %get-tuple-element.29), channel_id=1, source_target_pairs={{0,96},{16,112},{32,0},{48,16},{64,32},{80,48},{96,64},{112,80},{1... | collective-permute-start | bytes 786440 | tf_op jit(solution)/shard_map/ppermute | solution.py:437
  28.6 11.8 %collective-permute-start.6 = (f32[16,4,4,256]{3,2,1,0:T(4,128)S(1)}, f32[16,4,4,256]{3,2,1,0:T(4,128)S(1)}, u32[]{:S(2)}, u32[]{:S(2)}) collective-permute-start(f32[16,4,4,256]{3,2,1,0:T(4,128)S(1)} %collective-permute-done.2.high_ref), channel_id=1, source_target_pairs={{0,96},{16,112},{32,0},{48,16},{64,32},{80,48},{96,64},{112,80},{1... | collective-permute-start | bytes 786440 | tf_op jit(solution)/shard_map/ppermute | solution.py:438
  31.9 11.0 %collective-permute-start.5 = (f32[16,4,4,256]{3,2,1,0:T(4,128)S(1)}, f32[16,4,4,256]{3,2,1,0:T(4,128)S(1)}, u32[]{:S(2)}, u32[]{:S(2)}) collective-permute-start(f32[16,4,4,256]{3,2,1,0:T(4,128)S(1)} %collective-permute-done.1.low_ref), channel_id=1, source_target_pairs={{0,32},{16,48},{32,64},{48,80},{64,96},{80,112},{96,0},{112,16},{1... | collective-permute-start | bytes 786440 | tf_op jit(solution)/shard_map/ppermute | solution.py:438
  32.0 16.9 %copy-start.1 = (s32[2,16,6]{1,0,2:T(2,128)S(1)}, s32[2,16,6]{1,0,2:T(2,128)}, u32[]{:S(2)}) copy-start(s32[2,16,6]{1,0,2:T(2,128)} %param.13) | copy-start | bytes 2308
  44.7 5.8 %collective-permute-start.7 = (f32[2,16,4,1024]{3,2,1,0:T(4,128)S(1)}, f32[2,16,4,1024]{3,2,1,0:T(4,128)}, u32[]{:S(2)}, u32[]{:S(2)}) collective-permute-start(f32[2,16,4,1024]{3,2,1,0:T(4,128)S(1)} %last.3), channel_id=1, source_target_pairs={{0,16},{16,0},{32,48},{48,32},{64,80},{80,64},{96,112},{112,96},{1... | collective-permute-start | bytes 1572872 | tf_op jit(solution)/shard_map/ppermute | solution.py:452
  55.0 35.0 %all-to-all-start.1 = ((f32[16,280,128]{2,1,0:T(8,128)}), f32[16,280,128]{2,1,0:T(8,128)S(1)}, u32[]{:S(2)}, u32[]{:S(2)}) async-start(f32[16,280,128]{2,1,0:T(8,128)} %select.1), calls=%async_computation.1 | async-start | bytes 4587520 | tf_op jit(solution)/shard_map/all_to_all | solution.py:455
where the time goes:
time: 96.4 us; the launch traced here: 95.7 us
  waiting for transfers between devices  46 us (48%)
  starting transfers between devices  26 us (27%)
  Pallas kernels  21.7 us (23%)
  local copies, waits for them, and re-layouts  1.1 us (1%)
    all_to_all x1, waiting for transfers between devices, per_device(): got = lax.all_to_all(message, 'col', 0, 0, tiled=True)  31.1 us
    all_to_all x1, starting transfers between devices, per_device(): shard = lax.all_to_all(pack(root_inverse), 'col', 0, 0, tiled=True)  8.61 us
    all_to_all x1, waiting for transfers between devices, per_device(): shard = lax.all_to_all(pack(root_inverse), 'col', 0, 0, tiled=True)  8.24 us
    pallas_call x3, Pallas kernels, fill(): pl.pallas_call(functools.partial(fill_kernel, whence), out_shape=(jax.Sha...  6.5 us
    pallas_call x1, Pallas kernels, finish(): pl.pallas_call(final_kernel, out_shape=tuple((pltpu.HBM(shape, F32) for s...  5.68 us
    ppermute x2, starting transfers between devices, per_device(): ahead = [lax.ppermute(half, 'row', BACKWARD) for half in halves]  4.99 us
    pallas_call x1, Pallas kernels, select(): pl.pallas_call(select_kernel, out_shape=pltpu.HBM((COLS, MESSAGE, 128), F...  4.39 us
    ppermute x1, starting transfers between devices, per_device(): other = lax.ppermute(other, 'row', SWAP)  4.14 us
  transfers between devices with their start and end apart: 10, of which 7 were waited for; matrix products, arithmetic and copies ran while one was open for 0% of the time, Pallas kernels for 8%

commit v1 on v0

--- a/solution.py
+++ b/solution.py
@@ -188,11 +188,13 @@
                         lanes = slice(pair * 128, pair * 128 + 128)
                         out[parent, a, :, lanes] = jnp.where(left_half, halves[0], halves[1])
 
-                for (place, half), piece in zip(whence, pieces):
-
-                    @pl.when(here & (step == place) & (high == half))
-                    def _():
-                        fill(piece)
+                @pl.when(here)
+                def _():
+                    for (place, half), piece in zip(whence, pieces):
+
+                        @pl.when((step == place) & (high == half))
+                        def _():
+                            fill(piece)
 
         return carry
 
@@ -220,19 +222,26 @@
     for parent in range(2):
         for a in range(ONE):
             here = source_of(place_ref, one_ref[parent, a])[1]
-            for pair in range(ONE // 2):
-                lanes = slice(pair * 128, pair * 128 + 128)
+            for tile in range(ONE // 2):
+                lanes = slice(tile * 128, tile * 128 + 128)
                 value = jnp.where(
                     here, mine_ref[parent, a, :, lanes], other_ref[parent, a, :, lanes]
                 )
-                band[0, parent, a, :, lanes] = value
-                band[1, parent, a, :, lanes] = pltpu.roll(value, BLOCK, 1)
+                at = (parent * 8 + tile) * ONE + a
+                band[at] = value
+                band[256 + at] = pltpu.roll(value, BLOCK, 1)
+
+    def rows_of(parent):
+        tiles = [
+            band[(parent * 8 + tile) * ONE : (parent * 8 + tile + 1) * ONE].reshape(BAND, 128)
+            for tile in range(ONE // 2)
+        ]
+        return jnp.concatenate(tiles, axis=1)
+
     columns = jnp.concatenate(
         [
             -product(
-                split(band[0, parent].reshape(BAND, ONE * BLOCK)),
-                (high_ref[parent], low_ref[parent]),
-                ((1,), (1,)),
+                split(rows_of(parent)), (high_ref[parent], low_ref[parent]), ((1,), (1,))
             )
             for parent in range(2)
         ],
@@ -256,12 +265,15 @@
             [jnp.maximum(two_ref[parent, child, n] - OWN, 0) for n in range(TWO)]
             for parent in range(2)
         ]
+        places = [
+            [
+                256 * ((block & 1) ^ parent) + 128 * parent + ((block >> 1) << 4)
+                for block in picks[parent]
+            ]
+            for parent in range(2)
+        ]
         for unit, (k, m) in enumerate(UNITS):
-            halves = []
-            for parent in range(2):
-                row, block = picks[parent][k], picks[parent][m]
-                lanes = pl.ds(pl.multiple_of((block >> 1) << 7, 128), 128)
-                halves.append(band[(block & 1) ^ parent, parent, row, :, lanes])
+            halves = [band[picks[parent][k] + places[parent][m]] for parent in range(2)]
             top = CHILD_TOP + unit * SLICE
             ready[child, top : top + SLICE, :] = jnp.where(left_half, halves[0], halves[1])
         return carry
@@ -282,7 +294,7 @@
         in_specs=[SMEM] * 3 + [VMEM] * 4,
         out_specs=HBM,
         scratch_shapes=[
-            pltpu.VMEM((2,) + ROWS_SHAPE, F32),
+            pltpu.VMEM((512, SLICE, 128), F32),
             pltpu.VMEM((COLS, MESSAGE, 128), F32),
             pltpu.SemaphoreType.DMA((3,)),
         ],
@@ -291,11 +303,12 @@
     )(place, pattern_one, pattern_two, high, low, mine, other)
 
 
-def final_kernel(two_ref, got_ref, *refs):
+def final_kernel(place_ref, two_ref, got_ref, *refs):
     (far_in, far_out, beside, chosen, near_in, near_out, sems) = (
         refs[:4], refs[4:8], refs[8:10], refs[10:12], refs[12:16], refs[16:20], refs[20],
     )
-    factor_ref, child_factor_ref, pivot_ref, child_pivot_ref = near_in
+    factor_ref, _, _, child_pivot_ref = near_in
+    child_factor_ref, pivot_ref = far_in[1:3]
     column_ref, diagonal_ref, child_column_ref, child_diagonal_ref = near_out
     fetches = [
         pltpu.make_async_copy(far, near, sems.at[n])
@@ -308,8 +321,7 @@
         ]
         for n, (far, near) in enumerate(zip(far_out, near_out))
     ]
-    for fetch in fetches:
-        fetch.start()
+    fetches[0].start()
     left_half = lax.broadcasted_iota(jnp.int32, (16, 128), 1) < BLOCK
     left_block = lax.broadcasted_iota(jnp.int32, (BLOCK, 128), 1) < BLOCK
     nt = ((1,), (1,))
@@ -321,6 +333,7 @@
         beside[0][here, 128:256] = tiles[1]
         beside[1][here, 0:128] = jnp.where(left_half, turned[0], turned[1])
         beside[1][here, 128:256] = turned[1]
+    fetches[3].start()
     for parent in range(2):
         column_ref[parent] = beside[parent][WIDTH:, 0:WIDTH].T
         stores[0][parent].start()
@@ -334,7 +347,6 @@
             chosen[m % 2][here, lanes] = value[:, half]
             chosen[1 - m % 2][here, lanes] = turned[:, half]
     fetches[0].wait()
-    fetches[2].wait()
     diagonals = [
         pivot_ref[parent]
         - product(split(factor_ref[parent]), split(beside[parent][WIDTH:, 0:WIDTH]))
@@ -348,7 +360,7 @@
     row_block = lax.broadcasted_iota(jnp.int32, (WIDE, WIDE), 0) // BLOCK
     lane_block = lax.broadcasted_iota(jnp.int32, (WIDE, WIDE), 1) // BLOCK
     for parent in range(2):
-        picks = [two_ref[parent, n] for n in range(TWO)]
+        picks = [two_ref[parent, place_ref[2], n] for n in range(TWO)]
         for k in range(TWO):
             here = slice(BLOCK * k, BLOCK * k + BLOCK)
             rows = pl.ds(pl.multiple_of(picks[k] << 6, BLOCK), BLOCK)
@@ -369,7 +381,6 @@
                 chosen[parent][here, 128:256] = jnp.where(
                     left_block & (picks[2] < OWN), tiles[1], near
                 )
-    fetches[1].wait()
     fetches[3].wait()
     factors = [split(child_factor_ref[parent, 0]) for parent in range(2)]
     results = []
@@ -394,7 +405,7 @@
             store.wait()
 
 
-def finish(own_two, got, arrays):
+def finish(place, pattern_two, got, arrays):
     shapes = (
         (2, WIDTH, ONE * BLOCK),
         (2, WIDTH, WIDTH),
@@ -404,7 +415,7 @@
     return pl.pallas_call(
         final_kernel,
         out_shape=tuple(pltpu.HBM(shape, F32) for shape in shapes),
-        in_specs=[SMEM, VMEM] + [HBM] * 4,
+        in_specs=[SMEM, SMEM, VMEM] + [HBM, VMEM, VMEM, HBM],
         out_specs=(HBM,) * 4,
         scratch_shapes=[pltpu.VMEM((WIDTH + ONE * BLOCK, 256), F32)] * 2
         + [pltpu.VMEM((WIDE, WIDE), F32)] * 2
@@ -413,7 +424,7 @@
         + [pltpu.SemaphoreType.DMA((12,))],
         compiler_params=pltpu.CompilerParams(vmem_limit_bytes=24 * 2**20),
         name="finish",
-    )(own_two, got, *in_hbm(arrays))
+    )(place, pattern_two, got, *in_hbm(arrays[:1]), *arrays[1:3], *in_hbm(arrays[3:]))
 
 
 FORWARD = [(r, (r + 2) % ROWS) for r in range(ROWS)]
@@ -425,8 +436,8 @@
     root_inverse, factor_one, pivot_one, pattern_one, factor_two, pivot_two, pattern_two
 ):
     row = lax.axis_index("row")
-    place = jnp.stack([row >> 1, row & 1]).astype(jnp.int32)
     col = lax.axis_index("col")
+    place = jnp.stack([row >> 1, row & 1, col]).astype(jnp.int32)
     pattern_other = lax.ppermute(pattern_one, "row", SWAP)
     factor_one = jnp.swapaxes(factor_one, 1, 2)
     factor_two = jnp.swapaxes(factor_two, 2, 3)
@@ -453,9 +464,9 @@
     (mine,) = fill("last", relayed, place, (pattern_one,), (mine,), across)
     message = select(place, pattern_one, pattern_two, high, low, mine, other)
     got = lax.all_to_all(message, "col", 0, 0, tiled=True)
-    own_two = lax.dynamic_index_in_dim(pattern_two, col, 1, keepdims=False)
     column_one, diagonal_one, column_two, diagonal_two = finish(
-        own_two,
+        place,
+        pattern_two,
         got.reshape(COLS * MESSAGE, 128),
         (factor_one, factor_two, pivot_one, pivot_two),
     )

time: 96.4 us -> 93.3 us (0.968)
  blocking collectives: 0 us -> 33.6 us
  waiting for transfers between devices: 46 us -> 14.8 us
  starting transfers between devices: 26 us -> 21.7 us
    all_to_all x0 -> x1, blocking collectives: none -> 33.6 us  [per_device(): got = lax.all_to_all(message, 'col', 0, 0, tiled=True)]
    all_to_all x1 -> x0, waiting for transfers between devices: 31.1 us -> none  [per_device(): got = lax.all_to_all(message, 'col', 0, 0, tiled=True)]
    all_to_all x1 -> x0, starting transfers between devices: 3.73 us -> none  [per_device(): got = lax.all_to_all(message, 'col', 0, 0, tiled=True)]
  transfers between devices with their start and end apart: 10 -> 9, of which waited for: 7 -> 5; matrix products, arithmetic and copies ran while one was open for 0% -> 0% of each run, Pallas kernels for 8% -> 9%
where the time goes in v1:
time: 93.3 us; the launch traced here: 93 us
  blocking collectives  33.6 us (36%)
  starting transfers between devices  21.7 us (23%)
  Pallas kernels  21 us (23%)
  waiting for transfers between devices  14.8 us (16%)
  local copies, waits for them, and re-layouts  0.94 us (1%)
    all_to_all x1, blocking collectives, per_device(): got = lax.all_to_all(message, 'col', 0, 0, tiled=True)  33.6 us
    all_to_all x1, starting transfers between devices, per_device(): shard = lax.all_to_all(pack(root_inverse), 'col', 0, 0, tiled=True)  8.61 us
    all_to_all x1, waiting for transfers between devices, per_device(): shard = lax.all_to_all(pack(root_inverse), 'col', 0, 0, tiled=True)  8.24 us
    pallas_call x3, Pallas kernels, fill(): pl.pallas_call(functools.partial(fill_kernel, whence), out_shape=(jax.Sha...  6.37 us
    pallas_call x1, Pallas kernels, finish(): pl.pallas_call(final_kernel, out_shape=tuple((pltpu.HBM(shape, F32) for s...  5.38 us
    ppermute x2, starting transfers between devices, per_device(): ahead = [lax.ppermute(half, 'row', BACKWARD) for half in halves]  4.99 us
    pallas_call x1, Pallas kernels, select(): pl.pallas_call(select_kernel, out_shape=pltpu.HBM((COLS, MESSAGE, 128), F...  4.02 us
    ppermute x1, starting transfers between devices, per_device(): other = lax.ppermute(other, 'row', SWAP)  3.58 us
  transfers between devices with their start and end apart: 9, of which 5 were waited for; matrix products, arithmetic and copies ran while one was open for 0% of the time, Pallas kernels for 9%

profile of v1, /device:TPU:1, one launch (start us, length us, event | category | flops | bytes accessed | tf_op | source)
XLA Modules:
  0.0 93.0 jit_solution(16478163331150894072)
XLA Ops:
  0.6 0.0 copy-start.2
  0.6 1.9 %pack.1 = f32[16,8,4,256]{3,2,1,0:T(4,128)} custom-call(f32[512,256]{1,0:T(8,128)} %root_ref.1), custom_call_target="tpu_custom_call" | custom-call | tf_op jit(solution)/shard_map/pack/pallas_call | solution.py:75
  2.6 8.6 %all-to-all-start = ((f32[16,8,4,256]{3,2,1,0:T(4,128)}), f32[16,8,4,256]{3,2,1,0:T(4,128)S(1)}, u32[]{:S(2)}, u32[]{:S(2)}) async-start(f32[16,8,4,256]{3,2,1,0:T(4,128)} %pack.1), calls=%async_computation | async-start | bytes 1048576 | tf_op jit(solution)/shard_map/all_to_all | solution.py:444
  11.2 1.0 %collective-permute-start = (s32[2,16]{1,0:T(2,128)}, s32[2,16]{1,0:T(2,128)S(1)}, u32[]{:S(2)}, u32[]{:S(2)}) collective-permute-start(s32[2,16]{1,0:T(2,128)} %one_ref.3), channel_id=1, source_target_pairs={{0,16},{16,0},{32,48},{48,32},{64,80},{80,64},{96,112},{112,96},{1... | collective-permute-start | bytes 392 | tf_op jit(solution)/shard_map/ppermute | solution.py:441
  12.2 1.0 %collective-permute-done.other_ref.refs_1_.refs_0_ = s32[2,16]{1,0:T(2,128)S(1)} collective-permute-done((s32[2,16]{1,0:T(2,128)}, s32[2,16]{1,0:T(2,128)S(1)}, u32[]{:S(2)}, u32[]{:S(2)}) %collective-permute-start) | collective-permute-done | bytes 160 | tf_op jit(solution)/shard_map/ppermute | solution.py:441
  13.3 8.2 %all-to-all-done.own_ref = f32[16,8,4,256]{3,2,1,0:T(4,128)S(1)} async-done(((f32[16,8,4,256]{3,2,1,0:T(4,128)}), f32[16,8,4,256]{3,2,1,0:T(4,128)S(1)}, u32[]{:S(2)}, u32[]{:S(2)}) %all-to-all-start) | async-done | bytes 524320 | tf_op jit(solution)/shard_map/all_to_all | solution.py:444
  21.5 0.8 fusion
  22.3 2.5 %collective-permute-start.2 = (f32[16,4,4,256]{3,2,1,0:T(4,128)}, f32[16,4,4,256]{3,2,1,0:T(4,128)S(1)}, u32[]{:S(2)}, u32[]{:S(2)}) collective-permute-start(f32[16,4,4,256]{3,2,1,0:T(4,128)} %get-tuple-element.28), channel_id=1, source_target_pairs={{0,96},{16,112},{32,0},{48,16},{64,32},{80,48},{96,64},{112,80},{1... | collective-permute-start | bytes 786440 | tf_op jit(solution)/shard_map/ppermute | solution.py:448
  24.8 0.0 collective-permute-start.1
  24.8 0.2 collective-permute-start.4
  25.0 2.5 %collective-permute-start.3 = (f32[16,4,4,256]{3,2,1,0:T(4,128)}, f32[16,4,4,256]{3,2,1,0:T(4,128)}, u32[]{:S(2)}, u32[]{:S(2)}) collective-permute-start(f32[16,4,4,256]{3,2,1,0:T(4,128)} %get-tuple-element.29), channel_id=1, source_target_pairs={{0,96},{16,112},{32,0},{48,16},{64,32},{80,48},{96,64},{112,80},{1... | collective-permute-start | bytes 786440 | tf_op jit(solution)/shard_map/ppermute | solution.py:448
  27.5 1.1 %collective-permute-done.2.high_ref = f32[16,4,4,256]{3,2,1,0:T(4,128)S(1)} collective-permute-done((f32[16,4,4,256]{3,2,1,0:T(4,128)}, f32[16,4,4,256]{3,2,1,0:T(4,128)S(1)}, u32[]{:S(2)}, u32[]{:S(2)}) %collective-permute-start.2) | collective-permute-done | bytes 262176 | tf_op jit(solution)/shard_map/ppermute | solution.py:448
  28.6 3.3 %collective-permute-start.6 = (f32[16,4,4,256]{3,2,1,0:T(4,128)S(1)}, f32[16,4,4,256]{3,2,1,0:T(4,128)S(1)}, u32[]{:S(2)}, u32[]{:S(2)}) collective-permute-start(f32[16,4,4,256]{3,2,1,0:T(4,128)S(1)} %collective-permute-done.2.high_ref), channel_id=1, source_target_pairs={{0,96},{16,112},{32,0},{48,16},{64,32},{80,48},{96,64},{112,80},{1... | collective-permute-start | bytes 786440 | tf_op jit(solution)/shard_map/ppermute | solution.py:449
  31.9 0.0 collective-permute-done.1.low_ref
  31.9 0.0 collective-permute-start.5
  31.9 0.1 pad_add_fusion.place_ref
  32.0 0.0 copy-done.2
  32.0 0.0 copy-start.3
  32.0 3.3 %early.1 = (f32[2,16,4,1024]{3,2,1,0:T(4,128)S(1)}, f32[2,16,4,1024]{3,2,1,0:T(4,128)S(1)}, bf16[2,192,1024]{2,1,0:T(8,128)(2,1)S(1)}, bf16[2,192,1024]{2,1,0:T(8,128)(2,1)S(1)}) custom-call(s32[3]{0:T(128)S(1)} %pad_add_fusion.place_ref, s32[2,16]{1,0:T(2,128)S(1)} %copy-done.2, s32[2,16]{1,0:T(2,128)S(1)} %collective-permute-done.other_ref.refs_1_.refs_0_, ...), custom_call_target="tpu_custom_call" | custom-call | bytes 12582912 | tf_op jit(solution)/shard_map/early/pallas_call | solution.py:151
  35.3 1.9 %collective-permute-done.4.refs_5_ = f32[16,4,4,256]{3,2,1,0:T(4,128)S(1)} collective-permute-done((f32[16,4,4,256]{3,2,1,0:T(4,128)}, f32[16,4,4,256]{3,2,1,0:T(4,128)S(1)}, u32[]{:S(2)}, u32[]{:S(2)}) %collective-permute-start.4) | collective-permute-done | bytes 262176 | tf_op jit(solution)/shard_map/ppermute | solution.py:447
  37.2 0.0 collective-permute-done.3.refs_4_
  37.2 3.0 %second.1 = (f32[2,16,4,1024]{3,2,1,0:T(4,128)S(1)}, f32[2,16,4,1024]{3,2,1,0:T(4,128)S(1)}) custom-call(s32[3]{0:T(128)S(1)} %pad_add_fusion.place_ref, s32[2,16]{1,0:T(2,128)S(1)} %copy-done.2, s32[2,16]{1,0:T(2,128)S(1)} %collective-permute-done.other_ref.refs_1_.refs_0_, f32[2,16,4,1024]{3,2,1,0:T(4,128)S(1)} %get-tuple-element.20.refs_2_, ...), custom_call_target="tpu_custom_call" | custom-call | bytes 3145728 | tf_op jit(solution)/shard_map/second/pallas_call | solution.py:206
  40.2 0.0 collective-permute-done.6.refs_3_
  40.2 2.6 %collective-permute-done.5.refs_2_ = f32[16,4,4,256]{3,2,1,0:T(4,128)S(1)} collective-permute-done((f32[16,4,4,256]{3,2,1,0:T(4,128)S(1)}, f32[16,4,4,256]{3,2,1,0:T(4,128)S(1)}, u32[]{:S(2)}, u32[]{:S(2)}) %collective-permute-start.5) | collective-permute-done | bytes 262176 | tf_op jit(solution)/shard_map/ppermute | solution.py:449
  42.8 1.5 %last.3 = f32[2,16,4,1024]{3,2,1,0:T(4,128)S(1)} custom-call(s32[3]{0:T(128)S(1)} %pad_add_fusion.place_ref, s32[2,16]{1,0:T(2,128)S(1)} %collective-permute-done.other_ref.refs_1_.refs_0_, f32[2,16,4,1024]{3,2,1,0:T(4,128)S(1)} %get-tuple-element.23.refs_1_, f32[16,4,4,256]{3,2,1,0:T(4,128)S(1)} %collective-permute-done.5.refs_2_, ...), custom_call_target="tpu_custom_call" | custom-call | bytes 3145728 | tf_op jit(solution)/shard_map/last/pallas_call | solution.py:206
  44.4 3.6 %collective-permute-start.7 = (f32[2,16,4,1024]{3,2,1,0:T(4,128)S(1)}, f32[2,16,4,1024]{3,2,1,0:T(4,128)}, u32[]{:S(2)}, u32[]{:S(2)}) collective-permute-start(f32[2,16,4,1024]{3,2,1,0:T(4,128)S(1)} %last.3), channel_id=1, source_target_pairs={{0,16},{16,0},{32,48},{48,32},{64,80},{80,64},{96,112},{112,96},{1... | collective-permute-start | bytes 1572872 | tf_op jit(solution)/shard_map/ppermute | solution.py:463
  48.0 0.0 copy-done.3
  48.0 0.1 copy.12.two_ref
  48.1 1.8 %last.2.mine_ref = f32[2,16,4,1024]{3,2,1,0:T(4,128)S(1)} custom-call(s32[3]{0:T(128)S(1)} %pad_add_fusion.place_ref, s32[2,16]{1,0:T(2,128)S(1)} %copy-done.2, f32[2,16,4,1024]{3,2,1,0:T(4,128)S(1)} %get-tuple-element.22.refs_1_, f32[16,4,4,256]{3,2,1,0:T(4,128)S(1)} %collective-permute-done.5.refs_2_, f32[16,4,4,256]{3,2,1,0:T(4,128)S(1)} %collective-permute-done.6.refs_3_), custom_call_target="tpu_custom_call" | custom-call | bytes 3145728 | tf_op jit(solution)/shard_map/last/pallas_call | solution.py:206
  49.9 0.0 collective-permute-done.7.other_ref
  49.9 4.0 %select.1 = f32[16,280,128]{2,1,0:T(8,128)} custom-call(s32[3]{0:T(128)S(1)} %pad_add_fusion.place_ref, s32[2,16]{1,0:T(2,128)S(1)} %copy-done.2, s32[2,16,6]{2,1,0:T(8,128)S(1)} %copy.12.two_ref, bf16[2,192,1024]{2,1,0:T(8,128)(2,1)S(1)} %get-tuple-element.18.high_ref, bf16[2,192,1024]{2,1,0:T(8,128)(2,1)S(1)} %get-tuple-element.19.low_ref, ...), custom_call_target="tpu_custom_call" | custom-call | tf_op jit(solution)/shard_map/select/pallas_call | solution.py:291
  53.9 0.0 copy-start
  53.9 0.0 copy-start.1
  54.0 33.6 %all_to_all.10 = f32[16,280,128]{2,1,0:T(8,128)S(1)} all-to-all(f32[16,280,128]{2,1,0:T(8,128)} %select.1), channel_id=1, replica_groups=mesh['row'=8,'col'=16] {'col'}, dimensions={0} | all-to-all | bytes 4587520 | tf_op jit(solution)/shard_map/all_to_all | solution.py:466
  87.6 0.0 copy-done
  87.6 0.0 copy-done.1
  87.6 5.4 %finish.1 = (f32[2,192,1024]{2,1,0:T(8,128)}, f32[2,192,192]{2,1,0:T(8,128)}, f32[2,1,192,384]{3,2,1,0:T(8,128)}, f32[2,1,192,192]{3,2,1,0:T(8,128)}) custom-call(s32[3]{0:T(128)S(1)} %pad_add_fusion.place_ref, s32[2,16,6]{2,1,0:T(8,128)S(1)} %copy.12.two_ref, f32[4480,128]{1,0:T(8,128)S(1)} %bitcast.8, f32[2,192,1024]{2,1,0:T(8,128)} %bitcast.11, ...), custom_call_target="tpu_custom_call" | custom-call | tf_op jit(solution)/shard_map/finish/pallas_call | solution.py:415
Async XLA Ops:
  0.6 31.3 %copy-start.2 = (s32[2,16]{1,0:T(2,128)S(1)}, s32[2,16]{1,0:T(2,128)}, u32[]{:S(2)}) copy-start(s32[2,16]{1,0:T(2,128)} %one_ref.3) | copy-start | bytes 388
  2.6 18.9 %all-to-all-start = ((f32[16,8,4,256]{3,2,1,0:T(4,128)}), f32[16,8,4,256]{3,2,1,0:T(4,128)S(1)}, u32[]{:S(2)}, u32[]{:S(2)}) async-start(f32[16,8,4,256]{3,2,1,0:T(4,128)} %pack.1), calls=%async_computation | async-start | bytes 1048576 | tf_op jit(solution)/shard_map/all_to_all | solution.py:444
  11.2 2.1 %collective-permute-start = (s32[2,16]{1,0:T(2,128)}, s32[2,16]{1,0:T(2,128)S(1)}, u32[]{:S(2)}, u32[]{:S(2)}) collective-permute-start(s32[2,16]{1,0:T(2,128)} %one_ref.3), channel_id=1, source_target_pairs={{0,16},{16,0},{32,48},{48,32},{64,80},{80,64},{96,112},{112,96},{1... | collective-permute-start | bytes 392 | tf_op jit(solution)/shard_map/ppermute | solution.py:441
  22.3 6.2 %collective-permute-start.2 = (f32[16,4,4,256]{3,2,1,0:T(4,128)}, f32[16,4,4,256]{3,2,1,0:T(4,128)S(1)}, u32[]{:S(2)}, u32[]{:S(2)}) collective-permute-start(f32[16,4,4,256]{3,2,1,0:T(4,128)} %get-tuple-element.28), channel_id=1, source_target_pairs={{0,96},{16,112},{32,0},{48,16},{64,32},{80,48},{96,64},{112,80},{1... | collective-permute-start | bytes 786440 | tf_op jit(solution)/shard_map/ppermute | solution.py:448
  24.8 7.1 %collective-permute-start.1 = (f32[16,4,4,256]{3,2,1,0:T(4,128)}, f32[16,4,4,256]{3,2,1,0:T(4,128)S(1)}, u32[]{:S(2)}, u32[]{:S(2)}) collective-permute-start(f32[16,4,4,256]{3,2,1,0:T(4,128)} %get-tuple-element.29), channel_id=1, source_target_pairs={{0,32},{16,48},{32,64},{48,80},{64,96},{80,112},{96,0},{112,16},{1... | collective-permute-start | bytes 786440 | tf_op jit(solution)/shard_map/ppermute | solution.py:447
  24.8 12.4 %collective-permute-start.4 = (f32[16,4,4,256]{3,2,1,0:T(4,128)}, f32[16,4,4,256]{3,2,1,0:T(4,128)S(1)}, u32[]{:S(2)}, u32[]{:S(2)}) collective-permute-start(f32[16,4,4,256]{3,2,1,0:T(4,128)} %get-tuple-element.28), channel_id=1, source_target_pairs={{0,32},{16,48},{32,64},{48,80},{64,96},{80,112},{96,0},{112,16},{1... | collective-permute-start | bytes 786440 | tf_op jit(solution)/shard_map/ppermute | solution.py:447
  25.0 12.2 %collective-permute-start.3 = (f32[16,4,4,256]{3,2,1,0:T(4,128)}, f32[16,4,4,256]{3,2,1,0:T(4,128)}, u32[]{:S(2)}, u32[]{:S(2)}) collective-permute-start(f32[16,4,4,256]{3,2,1,0:T(4,128)} %get-tuple-element.29), channel_id=1, source_target_pairs={{0,96},{16,112},{32,0},{48,16},{64,32},{80,48},{96,64},{112,80},{1... | collective-permute-start | bytes 786440 | tf_op jit(solution)/shard_map/ppermute | solution.py:448
  28.6 11.7 %collective-permute-start.6 = (f32[16,4,4,256]{3,2,1,0:T(4,128)S(1)}, f32[16,4,4,256]{3,2,1,0:T(4,128)S(1)}, u32[]{:S(2)}, u32[]{:S(2)}) collective-permute-start(f32[16,4,4,256]{3,2,1,0:T(4,128)S(1)} %collective-permute-done.2.high_ref), channel_id=1, source_target_pairs={{0,96},{16,112},{32,0},{48,16},{64,32},{80,48},{96,64},{112,80},{1... | collective-permute-start | bytes 786440 | tf_op jit(solution)/shard_map/ppermute | solution.py:449
  31.9 11.0 %collective-permute-start.5 = (f32[16,4,4,256]{3,2,1,0:T(4,128)S(1)}, f32[16,4,4,256]{3,2,1,0:T(4,128)S(1)}, u32[]{:S(2)}, u32[]{:S(2)}) collective-permute-start(f32[16,4,4,256]{3,2,1,0:T(4,128)S(1)} %collective-permute-done.1.low_ref), channel_id=1, source_target_pairs={{0,32},{16,48},{32,64},{48,80},{64,96},{80,112},{96,0},{112,16},{1... | collective-permute-start | bytes 786440 | tf_op jit(solution)/shard_map/ppermute | solution.py:449
  32.0 16.0 %copy-start.3 = (s32[2,16,6]{1,0,2:T(2,128)S(1)}, s32[2,16,6]{1,0,2:T(2,128)}, u32[]{:S(2)}) copy-start(s32[2,16,6]{1,0,2:T(2,128)} %param.13) | copy-start | bytes 2308
  44.4 5.5 %collective-permute-start.7 = (f32[2,16,4,1024]{3,2,1,0:T(4,128)S(1)}, f32[2,16,4,1024]{3,2,1,0:T(4,128)}, u32[]{:S(2)}, u32[]{:S(2)}) collective-permute-start(f32[2,16,4,1024]{3,2,1,0:T(4,128)S(1)} %last.3), channel_id=1, source_target_pairs={{0,16},{16,0},{32,48},{48,32},{64,80},{80,64},{96,112},{112,96},{1... | collective-permute-start | bytes 1572872 | tf_op jit(solution)/shard_map/ppermute | solution.py:463
  53.9 33.6 %copy-start = (f32[2,1,384,192]{2,3,1,0:T(8,128)S(1)}, f32[2,1,384,192]{2,3,1,0:T(8,128)}, u32[]{:S(2)}) copy-start(f32[2,1,384,192]{2,3,1,0:T(8,128)} %param.11) | copy-start | bytes 1769476
  53.9 33.6 %copy-start.1 = (f32[2,192,192]{2,1,0:T(8,128)S(1)}, f32[2,192,192]{2,1,0:T(8,128)}, u32[]{:S(2)}) copy-start(f32[2,192,192]{2,1,0:T(8,128)} %refs_2_.1) | copy-start | bytes 884740
